TPU v7x, 128 devices: a whole 4x4x4 slice. The times are simulated.
128 devices in a mesh: section: 2 (over core), dp: 32 (over x, y, z_lo), tensor: 2 (over z_hi).
Axes of the slice: x: 4, y: 4, z: 4 (z_hi: 2, z_lo: 2; z = z_hi * 2 + z_lo), core: 2. Of those that a mesh axis runs over, the one named last changes fastest.
Arguments:
- embeddings: bfloat16 [128, 256, 768], P('dp'), may hold values from -6 to 6
- species: int32 [128], P('dp'), may hold values from 0 to 1
- ln1_gain: float32 [2, 768], P('section'), may hold values from 0.1 to 1.9
- ln1_bias: float32 [2, 768], P('section'), may hold values from -1.5 to 1.5
- qkv_weight: bfloat16 [2, 768, 3, 768], P('section', None, None, 'tensor'), may hold values from -0.21875 to 0.21875
- out_weight: bfloat16 [2, 768, 768], P('section', 'tensor'), may hold values from -0.625 to 0.625
- ln2_gain: float32 [2, 768], P('section'), may hold values from 0.1 to 1.9
- ln2_bias: float32 [2, 768], P('section'), may hold values from -1.5 to 1.5
- up_weight: bfloat16 [2, 768, 3072], P('section', None, 'tensor'), may hold values from -0.21875 to 0.21875
- up_bias: float32 [2, 3072], P('section', 'tensor'), may hold values from -3 to 3
- down_weight: bfloat16 [2, 3072, 768], P('section', 'tensor'), may hold values from -0.109375 to 0.109375
- species_bias: float32 [2, 2, 768], P('section'), may hold values from -3 to 3
- out_cotangent: float32 [128, 256, 768], P('dp'), may hold values from -6 to 6
Outputs:
- layer_out: float32 [2, 128, 256, 768], P('section', 'dp')
- input_grad: float32 [2, 128, 256, 768], P('section', 'dp')
- grad_ln1_gain: float32 [2, 768], P('section')
- grad_ln1_bias: float32 [2, 768], P('section')
- grad_qkv: float32 [2, 768, 3, 768], P('section', None, None, 'tensor')
- grad_out: float32 [2, 768, 768], P('section', 'tensor')
- grad_ln2_gain: float32 [2, 768], P('section')
- grad_ln2_bias: float32 [2, 768], P('section')
- grad_up: float32 [2, 768, 3072], P('section', None, 'tensor')
- grad_up_bias: float32 [2, 3072], P('section', 'tensor')
- grad_down: float32 [2, 3072, 768], P('section', 'tensor')
- grad_species: float32 [2, 2, 768], P('section')
All inputs are finite; a program needn't handle non-finite values.
Results may differ from a plain program's by a relative error of at most 0.024.
Values may be sent and summed in bfloat16 or wider, within the bound.
A program may use at most 320 MiB of HBM per device.

v0:
```python
import jax
import jax.numpy as jnp
from jax import lax
from jax.sharding import PartitionSpec as P

HEAD = 64


epsilon = 1e-05
root_half = 0.7071067811865476
density_scale = 0.3989422804014327


def shifted_2(block, axis, distance):
    devices = range(lax.axis_size(axis))
    route = [(i - distance, i) for i in devices if i - distance in devices]
    return lax.ppermute(block, axis, route)


def normalize(values):
    center = values - jnp.mean(values, axis=-1, keepdims=True)
    inverse = lax.rsqrt(jnp.mean(center * center, axis=-1, keepdims=True) + epsilon)
    return (center * inverse, inverse)


def norm_back(grad_normed, normed, inverse):
    return inverse * (
        grad_normed
        - jnp.mean(grad_normed, axis=-1, keepdims=True)
        - normed * jnp.mean(grad_normed * normed, axis=-1, keepdims=True)
    )


def gelu_slope(values):
    return 0.5 * (1.0 + lax.erf(values * root_half)) + values * density_scale * jnp.exp(
        -0.5 * values * values
    )


def row_inner(operand, against):
    return lax.dot_general(
        operand, against, (((0,), (0,)), ((), ())), preferred_element_type=jnp.float32
    )


def back_product(operand, against):
    return lax.dot_general(
        operand, against, (((1,), (1,)), ((), ())), preferred_element_type=jnp.float32
    )


def species_pick(table, species_flag):
    return (jnp.arange(table.shape[0]) == species_flag)[:, None]


def layer_forward(inputs, species_flag, weights):
    gain_one, bias_one, qkv_w, out_w, gain_two, bias_two, up_w, up_b, down_w, table = weights
    row_count = inputs.shape[0]
    local_width = out_w.shape[0]
    head_count = local_width // HEAD
    shifted = inputs + jnp.sum(jnp.where(species_pick(table, species_flag), table, 0.0), axis=0)
    normed_one, inverse_one = normalize(shifted)
    act_one = (normed_one * gain_one + bias_one).astype(jnp.bfloat16)
    projected = jnp.dot(
        act_one, qkv_w.reshape(qkv_w.shape[0], 3 * local_width), preferred_element_type=jnp.float32
    ).astype(jnp.bfloat16)
    queries = projected[:, :local_width].reshape(row_count, head_count, HEAD)
    key_vectors = projected[:, local_width : 2 * local_width].reshape(row_count, head_count, HEAD)
    value_vectors = projected[:, 2 * local_width :].reshape(row_count, head_count, HEAD)
    scores = jnp.einsum(
        "qhd,khd->hqk", queries, key_vectors, preferred_element_type=jnp.float32
    ) * HEAD ** (-0.5)
    row_max = jnp.max(scores, axis=-1, keepdims=True)
    log_total = row_max + jnp.log(jnp.sum(jnp.exp(scores - row_max), axis=-1, keepdims=True))
    attn_probs = jnp.exp(scores - log_total)
    head_mix = jnp.einsum(
        "hqk,khd->qhd",
        attn_probs.astype(jnp.bfloat16),
        value_vectors,
        preferred_element_type=jnp.float32,
    )
    head_mix = head_mix.astype(jnp.bfloat16).reshape(row_count, local_width)
    attention = lax.psum(
        jnp.dot(head_mix, out_w, preferred_element_type=jnp.float32).astype(jnp.bfloat16), "tensor"
    ).astype(jnp.float32)
    residual = shifted + attention
    normed_two, inverse_two = normalize(residual)
    act_two = (normed_two * gain_two + bias_two).astype(jnp.bfloat16)
    pre_act = jnp.dot(act_two, up_w, preferred_element_type=jnp.float32) + up_b
    hidden = jax.nn.gelu(pre_act, approximate=False).astype(jnp.bfloat16)
    unit_out = lax.psum(
        jnp.dot(hidden, down_w, preferred_element_type=jnp.float32).astype(jnp.bfloat16), "tensor"
    ).astype(jnp.float32)
    output = residual + unit_out
    kept_items = (
        normed_one,
        inverse_one,
        act_one,
        queries,
        key_vectors,
        value_vectors,
        log_total,
        head_mix,
        normed_two,
        inverse_two,
        act_two,
        pre_act,
        hidden,
    )
    return (output, kept_items)


def units_backward(grad_output, kept_items, weights):
    gain_two, up_w, down_w = (weights[4], weights[6], weights[8])
    normed_two, inverse_two, act_two, pre_act, hidden = (
        kept_items[8],
        kept_items[9],
        kept_items[10],
        kept_items[11],
        kept_items[12],
    )
    grad_branch = grad_output.astype(jnp.bfloat16)
    grad_down = row_inner(hidden, grad_branch)
    grad_pre = (back_product(grad_branch, down_w) * gelu_slope(pre_act)).astype(jnp.bfloat16)
    grad_up_b = jnp.sum(grad_pre, axis=0, dtype=jnp.float32)
    grad_up_w = row_inner(act_two, grad_pre)
    grad_act = lax.psum(back_product(grad_pre, up_w).astype(jnp.bfloat16), "tensor").astype(
        jnp.float32
    )
    grad_gain = jnp.sum(grad_act * normed_two, axis=0)
    grad_bias = jnp.sum(grad_act, axis=0)
    grad_resid = grad_output + norm_back(grad_act * gain_two, normed_two, inverse_two)
    return (grad_resid, (grad_gain, grad_bias, grad_up_w, grad_up_b, grad_down))


def heads_backward(grad_resid, kept_items, species_flag, weights):
    gain_one, qkv_w, out_w, table = (weights[0], weights[2], weights[3], weights[9])
    normed_one, inverse_one, act_one, queries, key_vectors, value_vectors, log_total, head_mix = (
        kept_items[:8]
    )
    row_count, head_count = (queries.shape[0], queries.shape[1])
    local_width = out_w.shape[0]
    score_scale = HEAD ** (-0.5)
    grad_attn = grad_resid.astype(jnp.bfloat16)
    grad_out_w = row_inner(head_mix, grad_attn)
    grad_mix = (
        back_product(grad_attn, out_w).astype(jnp.bfloat16).reshape(row_count, head_count, HEAD)
    )
    scores = (
        jnp.einsum("qhd,khd->hqk", queries, key_vectors, preferred_element_type=jnp.float32)
        * score_scale
    )
    attn_probs = jnp.exp(scores - log_total)
    grad_probs = jnp.einsum(
        "qhd,khd->hqk", grad_mix, value_vectors, preferred_element_type=jnp.float32
    )
    grad_values = jnp.einsum(
        "hqk,qhd->khd",
        attn_probs.astype(jnp.bfloat16),
        grad_mix,
        preferred_element_type=jnp.float32,
    ).astype(jnp.bfloat16)
    grad_scores = (
        attn_probs * (grad_probs - jnp.sum(attn_probs * grad_probs, axis=-1, keepdims=True))
    ).astype(jnp.bfloat16)
    grad_queries = (
        jnp.einsum("hqk,khd->qhd", grad_scores, key_vectors, preferred_element_type=jnp.float32)
        * score_scale
    ).astype(jnp.bfloat16)
    grad_keys = (
        jnp.einsum("hqk,qhd->khd", grad_scores, queries, preferred_element_type=jnp.float32)
        * score_scale
    ).astype(jnp.bfloat16)
    grad_proj = jnp.concatenate(
        [
            grad_queries.reshape(row_count, local_width),
            grad_keys.reshape(row_count, local_width),
            grad_values.reshape(row_count, local_width),
        ],
        axis=1,
    )
    grad_qkv = row_inner(act_one, grad_proj).reshape(qkv_w.shape)
    grad_act = lax.psum(
        back_product(grad_proj, qkv_w.reshape(qkv_w.shape[0], 3 * local_width)).astype(
            jnp.bfloat16
        ),
        "tensor",
    ).astype(jnp.float32)
    grad_gain = jnp.sum(grad_act * normed_one, axis=0)
    grad_bias = jnp.sum(grad_act, axis=0)
    grad_in = grad_resid + norm_back(grad_act * gain_one, normed_one, inverse_one)
    grad_table = jnp.where(
        species_pick(table, species_flag), jnp.sum(grad_in, axis=0)[None, :], 0.0
    )
    return (grad_in, (grad_gain, grad_bias, grad_qkv, grad_out_w, grad_table))


def shards(
    embeddings,
    species,
    ln1_gain,
    ln1_bias,
    qkv_weight,
    out_weight,
    ln2_gain,
    ln2_bias,
    up_weight,
    up_bias,
    down_weight,
    species_bias,
    out_cotangent,
):
    micro_count = embeddings.shape[0]
    row_count, model_width = (embeddings.shape[1], embeddings.shape[2])
    section_index = lax.axis_index("section")
    first_section = section_index == 0
    last_section = section_index == lax.axis_size("section") - 1
    weights = (
        ln1_gain[0],
        ln1_bias[0],
        qkv_weight[0],
        out_weight[0],
        ln2_gain[0],
        ln2_bias[0],
        up_weight[0],
        up_bias[0],
        down_weight[0],
        species_bias[0],
    )
    incoming = jnp.zeros((row_count, model_width), jnp.float32)
    outputs = []
    kept_ticks = []
    for tick_index in range(micro_count + 1):
        batch_index = jnp.clip(tick_index - section_index, 0, micro_count - 1)
        own_input = embeddings[min(tick_index, micro_count - 1)].astype(jnp.float32)
        inputs = jnp.where(first_section, own_input, incoming)
        species_flag = lax.dynamic_index_in_dim(species, batch_index, 0, keepdims=False)
        output, kept_items = layer_forward(inputs, species_flag, weights)
        outputs.append(output)
        kept_ticks.append(kept_items)
        if tick_index < micro_count:
            incoming = shifted_2(output.astype(jnp.bfloat16), "section", 1).astype(jnp.float32)
    layer_out = lax.dynamic_slice_in_dim(jnp.stack(outputs), section_index, micro_count, 0)[None]
    kept_stack = jax.tree.map(lambda *pieces: jnp.stack(pieces), *kept_ticks)
    unit_totals = (
        jnp.zeros(ln2_gain.shape[1:], jnp.float32),
        jnp.zeros(ln2_bias.shape[1:], jnp.float32),
        jnp.zeros(up_weight.shape[1:], jnp.float32),
        jnp.zeros(up_bias.shape[1:], jnp.float32),
        jnp.zeros(down_weight.shape[1:], jnp.float32),
    )
    head_totals = (
        jnp.zeros(ln1_gain.shape[1:], jnp.float32),
        jnp.zeros(ln1_bias.shape[1:], jnp.float32),
        jnp.zeros(qkv_weight.shape[1:], jnp.float32),
        jnp.zeros(out_weight.shape[1:], jnp.float32),
        jnp.zeros(species_bias.shape[1:], jnp.float32),
    )
    returning = jnp.zeros((row_count, model_width), jnp.float32)
    grad_ticks = []
    for tick_index in range(micro_count + 1):
        batch_index = tick_index - 1 + section_index
        is_valid = ((batch_index >= 0) & (batch_index < micro_count)).astype(jnp.float32)
        clipped = jnp.clip(batch_index, 0, micro_count - 1)
        own_grad = lax.dynamic_index_in_dim(out_cotangent, clipped, 0, keepdims=False)
        grad_output = jnp.where(last_section, own_grad, returning) * is_valid
        kept_items = jax.tree.map(
            lambda stacked: lax.dynamic_index_in_dim(
                stacked, clipped + section_index, 0, keepdims=False
            ),
            kept_stack,
        )
        species_flag = lax.dynamic_index_in_dim(species, clipped, 0, keepdims=False)
        grad_resid, unit_terms = units_backward(grad_output, kept_items, weights)
        unit_totals = jax.tree.map(jnp.add, unit_totals, unit_terms)
        grad_in, head_terms = heads_backward(grad_resid, kept_items, species_flag, weights)
        head_totals = jax.tree.map(jnp.add, head_totals, head_terms)
        grad_ticks.append(grad_in)
        if tick_index < micro_count:
            returning = shifted_2(grad_in.astype(jnp.bfloat16), "section", -1).astype(jnp.float32)
    input_grad = lax.dynamic_slice_in_dim(jnp.stack(grad_ticks), 1 - section_index, micro_count, 0)[
        None
    ]
    summed = lax.psum(
        (
            head_totals[0],
            head_totals[1],
            head_totals[2],
            head_totals[3],
            head_totals[4],
            unit_totals[0],
            unit_totals[1],
            unit_totals[2],
            unit_totals[3],
            unit_totals[4],
        ),
        "dp",
    )
    head_final = summed[:5]
    unit_final = summed[5:]
    return (
        layer_out,
        input_grad,
        head_final[0][None],
        head_final[1][None],
        head_final[2][None],
        head_final[3][None],
        unit_final[0][None],
        unit_final[1][None],
        unit_final[2][None],
        unit_final[3][None],
        unit_final[4][None],
        head_final[4][None],
    )


def solution(mesh):
    placed = (
        P("dp", None, None),
        P("dp"),
        P("section", None),
        P("section", None),
        P("section", None, None, "tensor"),
        P("section", "tensor", None),
        P("section", None),
        P("section", None),
        P("section", None, "tensor"),
        P("section", "tensor"),
        P("section", "tensor", None),
        P("section", None, None),
        P("dp", None, None),
    )
    return jax.shard_map(
        shards,
        mesh=mesh,
        in_specs=placed,
        out_specs=(
            P("section", "dp", None, None),
            P("section", "dp", None, None),
            P("section", None),
            P("section", None),
            P("section", None, None, "tensor"),
            P("section", "tensor", None),
            P("section", None),
            P("section", None),
            P("section", None, "tensor"),
            P("section", "tensor"),
            P("section", "tensor", None),
            P("section", None, None),
        ),
        check_vma=False,
    )
```

profile of v0, /device:TPU:0, one launch (start us, length us, event | category | flops | bytes accessed | tf_op | source)
XLA Modules:
  0.0 1581.8 jit_solution(7373205209590977334)
XLA Ops:
  7.3 4.0 copy.85
  32.6 28.9 %all-reduce.24.cloned.1.call-done = bf16[256,768]{1,0:T(8,128)(2,1)} async-done(((bf16[256,768]{1,0:T(8,128)(2,1)}), bf16[256,768]{1,0:T(8,128)(2,1)}) %all-reduce.24.cloned.1.call-update) | async-done | bytes 393232 | tf_op jit(solution)/shard_map/psum | solution.py:83
  64.4 6.5 bitcast_dynamic-update-slice_fusion.9
  77.5 28.2 %all-reduce.26.cloned.1.call-done = bf16[256,768]{1,0:T(8,128)(2,1)} async-done(((bf16[256,768]{1,0:T(8,128)(2,1)}), bf16[256,768]{1,0:T(8,128)(2,1)}) %all-reduce.26.cloned.1.call-update) | async-done | bytes 393232 | tf_op jit(solution)/shard_map/psum | solution.py:91
  129.7 23.8 %all-reduce.28.cloned.1.call-done = bf16[256,768]{1,0:T(8,128)(2,1)} async-done(((bf16[256,768]{1,0:T(8,128)(2,1)}), bf16[256,768]{1,0:T(8,128)(2,1)}) %all-reduce.28.cloned.1.call-update) | async-done | bytes 393232 | tf_op jit(solution)/shard_map/psum | solution.py:83
  155.2 5.1 bitcast_dynamic-update-slice_fusion.8
  165.6 29.5 %all-reduce.30.cloned.1.call-done = bf16[256,768]{1,0:T(8,128)(2,1)} async-done(((bf16[256,768]{1,0:T(8,128)(2,1)}), bf16[256,768]{1,0:T(8,128)(2,1)}) %all-reduce.30.cloned.1.call-update) | async-done | bytes 393232 | tf_op jit(solution)/shard_map/psum | solution.py:91
  220.9 23.6 %all-reduce.32.cloned.1.call-done = bf16[256,768]{1,0:T(8,128)(2,1)} async-done(((bf16[256,768]{1,0:T(8,128)(2,1)}), bf16[256,768]{1,0:T(8,128)(2,1)}) %all-reduce.32.cloned.1.call-update) | async-done | bytes 393232 | tf_op jit(solution)/shard_map/psum | solution.py:83
  246.2 5.1 bitcast_dynamic-update-slice_fusion.7
  256.6 29.5 %all-reduce.34.cloned.1.call-done = bf16[256,768]{1,0:T(8,128)(2,1)} async-done(((bf16[256,768]{1,0:T(8,128)(2,1)}), bf16[256,768]{1,0:T(8,128)(2,1)}) %all-reduce.34.cloned.1.call-update) | async-done | bytes 393232 | tf_op jit(solution)/shard_map/psum | solution.py:91
  311.8 23.8 %all-reduce.36.cloned.1.call-done = bf16[256,768]{1,0:T(8,128)(2,1)} async-done(((bf16[256,768]{1,0:T(8,128)(2,1)}), bf16[256,768]{1,0:T(8,128)(2,1)}) %all-reduce.36.cloned.1.call-update) | async-done | bytes 393232 | tf_op jit(solution)/shard_map/psum | solution.py:83
  337.3 5.1 bitcast_dynamic-update-slice_fusion.6
  347.7 29.5 %all-reduce.38.cloned.1.call-done = bf16[256,768]{1,0:T(8,128)(2,1)} async-done(((bf16[256,768]{1,0:T(8,128)(2,1)}), bf16[256,768]{1,0:T(8,128)(2,1)}) %all-reduce.38.cloned.1.call-update) | async-done | bytes 393232 | tf_op jit(solution)/shard_map/psum | solution.py:91
  406.8 19.5 %all-reduce.40.cloned.1.call-done = bf16[256,768]{1,0:T(8,128)(2,1)} async-done(((bf16[256,768]{1,0:T(8,128)(2,1)}), bf16[256,768]{1,0:T(8,128)(2,1)}) %all-reduce.40.cloned.1.call-update) | async-done | bytes 393232 | tf_op jit(solution)/shard_map/psum | solution.py:83
  428.0 5.1 bitcast_dynamic-update-slice_fusion.5
  435.3 3.3 convert_reduce_fusion.4
  443.9 30.4 %all-reduce.42.cloned.1.call-done = bf16[256,768]{1,0:T(8,128)(2,1)} async-done(((bf16[256,768]{1,0:T(8,128)(2,1)}), bf16[256,768]{1,0:T(8,128)(2,1)}) %all-reduce.42.cloned.1.call-update) | async-done | bytes 393232 | tf_op jit(solution)/shard_map/psum | solution.py:127
  490.0 3.4 fusion.143
  493.4 27.2 %all-reduce.44.cloned.1.call-done = bf16[256,768]{1,0:T(8,128)(2,1)} async-done(((bf16[256,768]{1,0:T(8,128)(2,1)}), bf16[256,768]{1,0:T(8,128)(2,1)}) %all-reduce.44.cloned.1.call-update) | async-done | bytes 393232 | tf_op jit(solution)/shard_map/psum | solution.py:183
  527.4 4.2 fusion.247
  531.6 4.1 fusion.310
  543.2 3.6 fusion.301
  546.8 29.3 %all-reduce.46.cloned.1.call-done = bf16[256,768]{1,0:T(8,128)(2,1)} async-done(((bf16[256,768]{1,0:T(8,128)(2,1)}), bf16[256,768]{1,0:T(8,128)(2,1)}) %all-reduce.46.cloned.1.call-update) | async-done | bytes 393232 | tf_op jit(solution)/shard_map/psum | solution.py:127
  594.3 4.0 fusion.308
  598.3 26.6 %all-reduce.48.cloned.1.call-done = bf16[256,768]{1,0:T(8,128)(2,1)} async-done(((bf16[256,768]{1,0:T(8,128)(2,1)}), bf16[256,768]{1,0:T(8,128)(2,1)}) %all-reduce.48.cloned.1.call-update) | async-done | bytes 393232 | tf_op jit(solution)/shard_map/psum | solution.py:183
  631.7 4.1 fusion.245
  640.3 3.1 convert_reduce_fusion.2
  646.9 3.5 fusion.299
  650.4 29.4 %all-reduce.50.cloned.1.call-done = bf16[256,768]{1,0:T(8,128)(2,1)} async-done(((bf16[256,768]{1,0:T(8,128)(2,1)}), bf16[256,768]{1,0:T(8,128)(2,1)}) %all-reduce.50.cloned.1.call-update) | async-done | bytes 393232 | tf_op jit(solution)/shard_map/psum | solution.py:127
  695.4 4.3 fusion.243
  699.7 4.0 fusion.306
  703.7 24.9 %all-reduce.52.cloned.1.call-done = bf16[256,768]{1,0:T(8,128)(2,1)} async-done(((bf16[256,768]{1,0:T(8,128)(2,1)}), bf16[256,768]{1,0:T(8,128)(2,1)}) %all-reduce.52.cloned.1.call-update) | async-done | bytes 393232 | tf_op jit(solution)/shard_map/psum | solution.py:183
  734.4 3.6 fusion.297
  748.8 4.0 fusion.304
  752.8 26.8 %all-reduce.54.cloned.1.call-done = bf16[256,768]{1,0:T(8,128)(2,1)} async-done(((bf16[256,768]{1,0:T(8,128)(2,1)}), bf16[256,768]{1,0:T(8,128)(2,1)}) %all-reduce.54.cloned.1.call-update) | async-done | bytes 393232 | tf_op jit(solution)/shard_map/psum | solution.py:127
  795.3 4.2 fusion.241
  801.8 26.7 %all-reduce.56.cloned.1.call-done = bf16[256,768]{1,0:T(8,128)(2,1)} async-done(((bf16[256,768]{1,0:T(8,128)(2,1)}), bf16[256,768]{1,0:T(8,128)(2,1)}) %all-reduce.56.cloned.1.call-update) | async-done | bytes 393232 | tf_op jit(solution)/shard_map/psum | solution.py:183
  833.7 3.7 fusion.295
  838.7 3.2 convert_reduce_fusion
  844.7 10.2 add_bitcast_fusion.1
  854.9 10.1 add_bitcast_fusion
  865.0 13.3 all-reduce.58.cloned.1.call-done
  894.5 8.0 add_bitcast_fusion.2
  910.8 22.7 %all-reduce.62.cloned.1.call-done = (bf16[256,768]{1,0:T(8,128)(2,1)}, bf16[256,768]{1,0:T(8,128)(2,1)}) async-done(((bf16[256,768]{1,0:T(8,128)(2,1)}, bf16[256,768]{1,0:T(8,128)(2,1)}), (bf16[256,768]{1,0:T(8,128)(2,1)}, bf16[256,768]{1,0:T(8,128)(2,1)})) %all-reduce.62.cloned.1.call-update) | async-done | bytes 786448 | tf_op jit(solution)/shard_map/psum | solution.py:91
  938.1 159.4 %all-reduce = (f32[1,768]{1,0:T(1,128)}, f32[1,768]{1,0:T(1,128)}, f32[1,768]{1,0:T(1,128)}, f32[1,768]{1,0:T(1,128)}, f32[1,1536]{1,0:T(1,128)}, /*index=5*/f32[1,2,768]{2,1,0:T(2,128)}) all-reduce(f32[1,768]{1,0:T(1,128)S(1)} %broadcast_in_dim.217, ...), channel_id=1, replica_groups=mesh['section'=2,'dp'=32,'tensor'=2] {'dp'}, use_global_device_ids=true, to_apply=%region_85.86 | all-reduce | flops 6144 | bytes 49152 | tf_op jit(solution)/shard_map/psum | solution.py:284
  1099.7 4.0 dynamic-slice_bitcast_fusion.1
  1105.7 458.0 %all-reduce.60.cloned.1.call-done = (f32[1,768,3,384]{3,1,2,0:T(8,128)}, f32[1,384,768]{2,1,0:T(8,128)}, f32[1,768,1536]{2,1,0:T(8,128)}, f32[1,1536,768]{2,1,0:T(8,128)}) async-done(((f32[1,768,3,384]{3,1,2,0:T(8,128)}, f32[1,384,768]{2,1,0:T(8,128)}, f32[1,768,1536]{2,1,0:T(8,128)}, f32[1,1536,768]{2,1,0:T(8,128)}), (f32[1,768,3,384]{3,1,2,0:T(8,128)}, f32[1,384,768]{2,1,0:T(8,128)}, ...) | async-done | bytes 14155792 | tf_op jit(solution)/shard_map/psum | solution.py:284
  1563.7 4.2 copy.260
  (741 shorter events, 325.9 us)
Async XLA Ops:
  7.2 57.1 %copy-start = (bf16[1,768,1536]{2,1,0:T(8,128)(2,1)S(1)}, bf16[1,768,1536]{2,1,0:T(8,128)(2,1)}, u32[]{:S(2)}) copy-start(bf16[1,768,1536]{2,1,0:T(8,128)(2,1)} %param.21) | copy-start | bytes 7077892
  7.2 54.3 %all-reduce.24.cloned.1.call-start = ((), (), s32[]{:S(2)}) async-start(), calls=%async_computation | async-start | bytes 786432 | tf_op jit(solution)/shard_map/psum | solution.py:83
  25.0 80.7 %all-reduce.26.cloned.1.call-start = ((), (), s32[]{:S(2)}) async-start(), calls=%async_computation.1 | async-start | bytes 786432 | tf_op jit(solution)/shard_map/psum | solution.py:91
  32.6 31.7 %copy-start.106 = (f32[768]{0:T(1024)S(1)}, f32[768]{0:T(1024)}, u32[]{:S(2)}) copy-start(f32[768]{0:T(1024)} %reduce.3) | copy-start | bytes 9220
  32.6 31.7 %copy-start.159 = (f32[1536]{0:T(1024)S(1)}, f32[1536]{0:T(1024)}, u32[]{:S(2)}) copy-start(f32[1536]{0:T(1024)} %reduce.4) | copy-start | bytes 18436
  72.4 81.1 %all-reduce.28.cloned.1.call-start = ((), (), s32[]{:S(2)}) async-start(), calls=%async_computation.2 | async-start | bytes 786432 | tf_op jit(solution)/shard_map/psum | solution.py:83
  107.1 5.6 collective-permute-start
  120.3 74.8 %all-reduce.30.cloned.1.call-start = ((), (), s32[]{:S(2)}) async-start(), calls=%async_computation.3 | async-start | bytes 786432 | tf_op jit(solution)/shard_map/psum | solution.py:91
  161.8 82.7 %all-reduce.32.cloned.1.call-start = ((), (), s32[]{:S(2)}) async-start(), calls=%async_computation.4 | async-start | bytes 786432 | tf_op jit(solution)/shard_map/psum | solution.py:83
  196.5 3.7 collective-permute-start.1
  211.3 74.8 %all-reduce.34.cloned.1.call-start = ((), (), s32[]{:S(2)}) async-start(), calls=%async_computation.5 | async-start | bytes 786432 | tf_op jit(solution)/shard_map/psum | solution.py:91
  252.9 82.8 %all-reduce.36.cloned.1.call-start = ((), (), s32[]{:S(2)}) async-start(), calls=%async_computation.6 | async-start | bytes 786432 | tf_op jit(solution)/shard_map/psum | solution.py:83
  287.5 3.8 collective-permute-start.2
  302.4 74.8 %all-reduce.38.cloned.1.call-start = ((), (), s32[]{:S(2)}) async-start(), calls=%async_computation.7 | async-start | bytes 786432 | tf_op jit(solution)/shard_map/psum | solution.py:91
  344.0 82.3 %all-reduce.40.cloned.1.call-start = ((), (), s32[]{:S(2)}) async-start(), calls=%async_computation.8 | async-start | bytes 786432 | tf_op jit(solution)/shard_map/psum | solution.py:83
  378.6 4.0 collective-permute-start.3
  393.1 81.2 %all-reduce.42.cloned.1.call-start = ((), (), s32[]{:S(2)}) async-start(), calls=%async_computation.9 | async-start | bytes 786432 | tf_op jit(solution)/shard_map/psum | solution.py:127
  441.1 79.6 %all-reduce.44.cloned.1.call-start = ((), (), s32[]{:S(2)}) async-start(), calls=%async_computation.10 | async-start | bytes 786432 | tf_op jit(solution)/shard_map/psum | solution.py:183
  487.4 88.6 %all-reduce.46.cloned.1.call-start = ((), (), s32[]{:S(2)}) async-start(), calls=%async_computation.11 | async-start | bytes 786432 | tf_op jit(solution)/shard_map/psum | solution.py:127
  490.0 32.9 %copy-start.175 = (f32[1,256,1]{1,2,0:T(1,128)S(1)}, f32[1,256,1]{1,2,0:T(1,128)}, u32[]{:S(2)}) copy-start(f32[1,256,1]{1,2,0:T(1,128)} %get-tuple-element.142) | copy-start | bytes 3076
  526.1 9.6 collective-permute-start.4
  542.1 82.8 %all-reduce.48.cloned.1.call-start = ((), (), s32[]{:S(2)}) async-start(), calls=%async_computation.12 | async-start | bytes 786432 | tf_op jit(solution)/shard_map/psum | solution.py:183
  543.2 35.1 %copy-start.179 = (f32[1,256,1]{1,2,0:T(1,128)S(1)}, f32[1,256,1]{1,2,0:T(1,128)}, u32[]{:S(2)}) copy-start(f32[1,256,1]{1,2,0:T(1,128)} %get-tuple-element.146) | copy-start | bytes 3076
  591.6 88.2 %all-reduce.50.cloned.1.call-start = ((), (), s32[]{:S(2)}) async-start(), calls=%async_computation.13 | async-start | bytes 786432 | tf_op jit(solution)/shard_map/psum | solution.py:127
  594.3 32.8 %copy-start.174 = (f32[1,256,1]{1,2,0:T(1,128)S(1)}, f32[1,256,1]{1,2,0:T(1,128)}, u32[]{:S(2)}) copy-start(f32[1,256,1]{1,2,0:T(1,128)} %get-tuple-element.141) | copy-start | bytes 3076
  630.1 8.2 collective-permute-start.5
  645.8 82.8 %all-reduce.52.cloned.1.call-start = ((), (), s32[]{:S(2)}) async-start(), calls=%async_computation.14 | async-start | bytes 786432 | tf_op jit(solution)/shard_map/psum | solution.py:183
  646.9 35.1 %copy-start.178 = (f32[1,256,1]{1,2,0:T(1,128)S(1)}, f32[1,256,1]{1,2,0:T(1,128)}, u32[]{:S(2)}) copy-start(f32[1,256,1]{1,2,0:T(1,128)} %get-tuple-element.145) | copy-start | bytes 3076
  695.4 84.2 %all-reduce.54.cloned.1.call-start = ((), (), s32[]{:S(2)}) async-start(), calls=%async_computation.15 | async-start | bytes 786432 | tf_op jit(solution)/shard_map/psum | solution.py:127
  699.7 31.1 %copy-start.173 = (f32[1,256,1]{1,2,0:T(1,128)S(1)}, f32[1,256,1]{1,2,0:T(1,128)}, u32[]{:S(2)}) copy-start(f32[1,256,1]{1,2,0:T(1,128)} %get-tuple-element.140) | copy-start | bytes 3076
  733.1 5.0 collective-permute-start.6
  745.6 82.9 %all-reduce.56.cloned.1.call-start = ((), (), s32[]{:S(2)}) async-start(), calls=%async_computation.16 | async-start | bytes 786432 | tf_op jit(solution)/shard_map/psum | solution.py:183
  748.8 32.9 %copy-start.177 = (f32[1,256,1]{1,2,0:T(1,128)S(1)}, f32[1,256,1]{1,2,0:T(1,128)}, u32[]{:S(2)}) copy-start(f32[1,256,1]{1,2,0:T(1,128)} %get-tuple-element.144) | copy-start | bytes 3076
  795.2 83.2 %all-reduce.58.cloned.1.call-start = ((), (), s32[]{:S(2)}) async-start(), calls=%async_computation.17 | async-start | bytes 786432 | tf_op jit(solution)/shard_map/psum | solution.py:127
  799.5 31.2 %copy-start.172 = (f32[1,256,1]{1,2,0:T(1,128)S(1)}, f32[1,256,1]{1,2,0:T(1,128)}, u32[]{:S(2)}) copy-start(f32[1,256,1]{1,2,0:T(1,128)} %get-tuple-element.139) | copy-start | bytes 3076
  832.3 5.1 collective-permute-start.7
  844.4 89.2 %all-reduce.62.cloned.1.call-start = ((), (), s32[]{:S(2)}) async-start(), calls=%async_computation.19 | async-start | bytes 1572864 | tf_op jit(solution)/shard_map/psum | solution.py:91
  854.9 25.6 %copy-start.176 = (f32[1,256,1]{1,2,0:T(1,128)S(1)}, f32[1,256,1]{1,2,0:T(1,128)}, u32[]{:S(2)}) copy-start(f32[1,256,1]{1,2,0:T(1,128)} %get-tuple-element.143) | copy-start | bytes 3076
  891.6 672.1 %all-reduce.60.cloned.1.call-start = ((), (), s32[]{:S(2)}) async-start(), calls=%async_computation.18 | async-start | bytes 28311552 | tf_op jit(solution)/shard_map/psum | solution.py:284
  908.5 26.7 %copy-start.124 = (f32[768]{0:T(1024)S(1)}, f32[768]{0:T(1024)}, u32[]{:S(2)}) copy-start(f32[768]{0:T(1024)} %get-tuple-element.24) | copy-start | bytes 9220
  908.5 26.7 %copy-start.128 = (f32[768]{0:T(1024)S(1)}, f32[768]{0:T(1024)}, u32[]{:S(2)}) copy-start(f32[768]{0:T(1024)} %get-tuple-element.22) | copy-start | bytes 9220
  908.5 26.7 %copy-start.132 = (f32[768]{0:T(1024)S(1)}, f32[768]{0:T(1024)}, u32[]{:S(2)}) copy-start(f32[768]{0:T(1024)} %get-tuple-element.26) | copy-start | bytes 9220
  908.6 26.7 %copy-start.135 = (f32[768]{0:T(1024)S(1)}, f32[768]{0:T(1024)}, u32[]{:S(2)}) copy-start(f32[768]{0:T(1024)} %get-tuple-element.28) | copy-start | bytes 9220
  908.6 26.7 %copy-start.123 = (f32[768]{0:T(1024)S(1)}, f32[768]{0:T(1024)}, u32[]{:S(2)}) copy-start(f32[768]{0:T(1024)} %get-tuple-element.48) | copy-start | bytes 9220
  908.6 26.7 %copy-start.127 = (f32[768]{0:T(1024)S(1)}, f32[768]{0:T(1024)}, u32[]{:S(2)}) copy-start(f32[768]{0:T(1024)} %get-tuple-element.47) | copy-start | bytes 9220
  908.6 26.7 %copy-start.131 = (f32[768]{0:T(1024)S(1)}, f32[768]{0:T(1024)}, u32[]{:S(2)}) copy-start(f32[768]{0:T(1024)} %get-tuple-element.49) | copy-start | bytes 9220
  908.6 26.7 %copy-start.171 = (f32[1,256,1]{1,2,0:T(1,128)S(1)}, f32[1,256,1]{1,2,0:T(1,128)}, u32[]{:S(2)}) copy-start(f32[1,256,1]{1,2,0:T(1,128)} %get-tuple-element.138) | copy-start | bytes 3076
  935.2 162.3 %copy-start.96 = (bf16[256,768]{1,0:T(8,128)(2,1)S(1)}, bf16[256,768]{1,0:T(8,128)(2,1)}, u32[]{:S(2)}) copy-start(bf16[256,768]{1,0:T(8,128)(2,1)} %get-tuple-element.67) | copy-start | bytes 1179652
  (173 other events, 734.7 us)
Sparse Core Ops, SparseCore 0:
  25.1 36.3 all-reduce.23
  72.6 33.0 all-reduce.25
  120.4 33.0 all-reduce.27
  162.0 33.0 all-reduce.29
  211.4 33.0 all-reduce.31
  253.0 33.0 all-reduce.33
  302.5 33.0 all-reduce.35
  344.1 33.0 all-reduce.37
  393.2 33.0 all-reduce.39
  441.2 33.0 all-reduce.41
  487.5 33.0 all-reduce.43
  542.2 33.8 all-reduce.45
  591.7 33.0 all-reduce.47
  645.9 33.8 all-reduce.49
  695.5 33.0 all-reduce.51
  745.7 33.8 all-reduce.53
  795.3 33.0 all-reduce.55
  844.5 33.8 all-reduce.57
  891.7 41.8 all-reduce.61
  937.6 626.0 all-reduce.59
where the time goes:
time: 1590 us; the launch traced here: 1580 us
  waiting for transfers between devices  952 us (60%)
  matrix products  208 us (13%)
  blocking collectives  159 us (10%)
  other arithmetic  117 us (7%)
  local copies, waits for them, and re-layouts  112 us (7%)
  between operations  17.2 us (1%)
    psum x1, waiting for transfers between devices, shards(): lax.psum((head_totals[0], head_totals[1], head_totals[2], head_totals[3],...  458 us
    psum x1, blocking collectives, shards(): lax.psum((head_totals[0], head_totals[1], head_totals[2], head_totals[3],...  159 us
    psum x5, waiting for transfers between devices, layer_forward(): lax.psum(jnp.dot(hidden, down_w, preferred_element_type=jnp.float32).asty...  139 us
    psum x5, waiting for transfers between devices, units_backward(): lax.psum(back_product(grad_pre, up_w).astype(jnp.bfloat16), 'tensor')  129 us
    psum x5, waiting for transfers between devices, layer_forward(): lax.psum(jnp.dot(head_mix, out_w, preferred_element_type=jnp.float32).ast...  120 us
    psum x4, waiting for transfers between devices, heads_backward(): lax.psum(back_product(grad_proj, qkv_w.reshape(qkv_w.shape[0], 3 * local_...  105 us
    dot_general x20, matrix products, row_inner(): lax.dot_general(operand, against, (((0,), (0,)), ((), ())), preferred_ele...  88.7 us
    unnamed x423, local copies, waits for them, and re-layouts  74 us
  transfers between devices with their start and end apart: 28, of which 20 were waited for; matrix products, arithmetic and copies ran while one was open for 12% of the time, Pallas kernels for 0%

commit v1 on v0

v1 whole, which is shorter than its diff:
```python
import functools

import jax
import jax.numpy as jnp
from jax import lax
from jax.experimental import pallas as pl
from jax.experimental.pallas import tpu as pltpu
from jax.sharding import PartitionSpec as P

HEAD = 64
BR, BC = 96, 384
MESH = pl.DeviceIdType.MESH
BF = jnp.bfloat16
F32 = jnp.float32

epsilon = 1e-05
root_half = 0.7071067811865476
density_scale = 0.3989422804014327


def place():
    dp = lax.axis_index("dp")
    z = lax.axis_index("tensor") * 2 + lax.rem(dp, 2)
    return dp // 8, lax.rem(dp // 2, 4), z, lax.axis_index("section")


def device(x, y, z, core):
    return (core, (x * 4 + y) * 2 + lax.rem(z, 2), z // 2)


def wrap(v):
    return lax.rem(v, 4)


def sum_kernel(g_ref, s_ref, full_ref, small_ref, r1, r2, r3, o1, s1, s2, s3, q1, q2, q3, ss, rs, qs, qr, ls, gs, gr, ws):
    x, y, z, c = place()
    t, zl = z // 2, lax.rem(z, 2)
    peers = []
    for k in (1, 2, 3):
        zk = wrap(z + k)
        other = lax.rem(zk // 2 + t, 2)
        peers.append(
            (
                (wrap(x + k), y, z, c),
                (x, wrap(y + k), z, c),
                (x, y, zk, lax.rem(c + other, 2)),
                other,
                wrap(x + k),
                wrap(y + k),
                lax.rem(zk, 2),
            )
        )
    barrier = pltpu.get_barrier_semaphore()
    for px, py, pz, *_ in peers:
        for p in (px, py, pz):
            pl.semaphore_signal(barrier, inc=1, device_id=device(*p), device_id_type=MESH)
    pl.semaphore_wait(barrier, 9)

    def send(src, dst, sems, rsems, idx, peer):
        cp = pltpu.make_async_remote_copy(
            src_ref=src, dst_ref=dst, send_sem=sems.at[idx], recv_sem=rsems.at[idx], device_id=device(*peer), device_id_type=MESH
        )
        cp.start()
        return cp

    own = c
    first = [[], [], []]
    for k in (1, 2, 3):
        px, py, pz, other, xk, yk, zlk = peers[k - 1]
        which = lax.rem(own + other, 2)
        first[0].append(
            [send(g_ref.at[which, 0, pl.ds(zlk * 16, 16)], r1.at[0, k - 1], ss, rs, (0, 0, k - 1, 0), pz)]
        )
        first[1].append(
            [send(g_ref.at[i, 1, pl.ds(xk * 8, 8)], r1.at[1, k - 1, pl.ds(i * 8, 8)], ss, rs, (0, 1, k - 1, i), px) for i in (0, 1)]
        )
        first[2].append(
            [send(g_ref.at[i, 2, pl.ds(yk * 8, 8)], r1.at[2, k - 1, pl.ds(i * 8, 8)], ss, rs, (0, 2, k - 1, i), py) for i in (0, 1)]
        )
    q1[pl.ds(x, 1)] = s_ref[...][None]
    small = [send(q1.at[x], q1.at[x], qs, qr, (0, k - 1), peers[k - 1][0]) for k in (1, 2, 3)]
    mine = [
        pltpu.make_async_copy(g_ref.at[own, 0, pl.ds(zl * 16, 16)], o1.at[0], ls.at[0]),
        pltpu.make_async_copy(g_ref.at[0, 1, pl.ds(x * 8, 8)], o1.at[1, pl.ds(0, 8)], ls.at[1]),
        pltpu.make_async_copy(g_ref.at[1, 1, pl.ds(x * 8, 8)], o1.at[1, pl.ds(8, 8)], ls.at[2]),
        pltpu.make_async_copy(g_ref.at[0, 2, pl.ds(y * 8, 8)], o1.at[2, pl.ds(0, 8)], ls.at[3]),
        pltpu.make_async_copy(g_ref.at[1, 2, pl.ds(y * 8, 8)], o1.at[2, pl.ds(8, 8)], ls.at[4]),
    ]
    for cp in mine:
        cp.start()
    for cp in mine:
        cp.wait()

    def add(dst, part, base, recv, count):
        @pl.loop(0, count)
        def _(i):
            total = base(i).astype(F32)
            for k in range(3):
                total += recv[part, k, pl.ds(i, 1)][0].astype(F32)
            dst[part, pl.ds(i, 1)] = total.astype(BF)[None]

    for cp in small:
        cp.wait()
    q2[pl.ds(y, 1)] = (((q1[0] + q1[1]) + q1[2]) + q1[3])[None]
    small = [send(q2.at[y], q2.at[y], qs, qr, (1, k - 1), peers[k - 1][1]) for k in (1, 2, 3)]
    second = [[], [], []]
    for p in range(3):
        for group in first[p]:
            for cp in group:
                cp.wait()
        add(s1, p, lambda i, p=p: o1[p, pl.ds(i, 1)][0], r1, 16)
        for k in (1, 2, 3):
            px, py, pz, other, xk, yk, zlk = peers[k - 1]
            which = lax.rem(own + other, 2)
            if p == 0:
                second[0].append([send(s1.at[0, pl.ds(xk * 4, 4)], r2.at[0, k - 1], ss, rs, (1, 0, k - 1, 0), px)])
            elif p == 1:
                second[1].append(
                    [
                        send(s1.at[1, pl.ds(i * 8 + yk * 2, 2)], r2.at[1, k - 1, pl.ds(i * 2, 2)], ss, rs, (1, 1, k - 1, i), py)
                        for i in (0, 1)
                    ]
                )
            else:
                second[2].append([send(s1.at[2, pl.ds(which * 8 + zlk * 4, 4)], r2.at[2, k - 1], ss, rs, (1, 2, k - 1, 0), pz)])
    for cp in small:
        cp.wait()
    q2sum = ((q2[0] + q2[1]) + q2[2]) + q2[3]
    q2[pl.ds(4, 1)] = q2sum[None]
    q3[pl.ds(z, 1)] = q2[4, pl.ds(own, 1)]
    small = []
    for k in (1, 2, 3):
        which = lax.rem(own + peers[k - 1][3], 2)
        small.append(send(q2.at[4, which], q3.at[z], qs, qr, (2, k - 1), peers[k - 1][2]))
    third = [[], [], []]
    bases = [
        lambda i: s1[0, pl.ds(x * 4 + i, 1)][0],
        lambda i: s1[1, pl.ds((i // 2) * 8 + y * 2 + lax.rem(i, 2), 1)][0],
        lambda i: s1[2, pl.ds(own * 8 + zl * 4 + i, 1)][0],
    ]
    for p in range(3):
        for group in second[p]:
            for cp in group:
                cp.wait()
        add(s2, p, bases[p], r2, 4)
        for k in (1, 2, 3):
            px, py, pz, other, xk, yk, zlk = peers[k - 1]
            which = lax.rem(own + other, 2)
            if p == 0:
                third[0].append(send(s2.at[0, yk], r3.at[0, k - 1, 0], ss, rs, (2, 0, k - 1, 0), py))
            elif p == 1:
                third[1].append(send(s2.at[1, which * 2 + zlk], r3.at[1, k - 1, 0], ss, rs, (2, 1, k - 1, 0), pz))
            else:
                third[2].append(send(s2.at[2, xk], r3.at[2, k - 1, 0], ss, rs, (2, 2, k - 1, 0), px))
    for cp in small:
        cp.wait()
    small_ref[...] = ((q3[0] + q3[1]) + q3[2]) + q3[3]
    bases = [
        lambda i: s2[0, pl.ds(y, 1)][0],
        lambda i: s2[1, pl.ds(own * 2 + zl, 1)][0],
        lambda i: s2[2, pl.ds(x, 1)][0],
    ]
    number = (zl * 16 + x * 4 + y, x * 8 + y * 2 + zl, y * 8 + zl * 4 + x)
    gather = [[], [], []]
    local = []

    def spread(p, step, start, count, axis):
        out = []
        for k in (1, 2, 3):
            if axis == 2 and k != 2:
                continue
            peer = peers[k - 1][axis] if axis < 2 else (x, y, t * 2 + 1 - zl, c)
            part = full_ref.at[p, pl.ds(start, count)]
            out.append(send(part, part, gs, gr, (p, step, k - 1), peer))
        return out

    for p in range(3):
        for cp in third[p]:
            cp.wait()
        add(s3, p, bases[p], r3, 1)
        cp = pltpu.make_async_copy(s3.at[p], full_ref.at[p, pl.ds(number[p], 1)], ws.at[p])
        cp.start()
        local.append(cp)
    orders = (
        ((1, number[0], 1), (0, zl * 16 + x * 4, 4), (2, zl * 16, 16)),
        ((2, number[1], 1), (1, x * 8 + y * 2, 2), (0, x * 8, 8)),
        ((0, number[2], 1), (2, y * 8 + zl * 4, 4), (1, y * 8, 8)),
    )
    for step in range(3):
        for p in range(3):
            if step == 0:
                local[p].wait()
            else:
                for cp in gather[p]:
                    cp.wait()
            axis, start, count = orders[p][step]
            gather[p] = spread(p, step, start, count, axis)
    for p in range(3):
        for cp in gather[p]:
            cp.wait()


def summed(grads, small):
    dma = pltpu.SemaphoreType.DMA
    blocks = lambda *lead: pltpu.VMEM((*lead, BR, BC), BF)
    anywhere = pl.BlockSpec(memory_space=pl.ANY)
    return pl.pallas_call(
        sum_kernel,
        out_shape=(jax.ShapeDtypeStruct((3, 32, BR, BC), BF), jax.ShapeDtypeStruct((8, 768), F32)),
        in_specs=[anywhere, pl.BlockSpec(memory_space=pltpu.VMEM)],
        out_specs=(anywhere, pl.BlockSpec(memory_space=pltpu.VMEM)),
        scratch_shapes=[
            blocks(3, 3, 16),
            blocks(3, 3, 4),
            blocks(3, 3, 1),
            blocks(3, 16),
            blocks(3, 16),
            blocks(3, 4),
            blocks(3, 1),
            pltpu.VMEM((4, 2, 8, 768), F32),
            pltpu.VMEM((5, 2, 8, 768), F32),
            pltpu.VMEM((4, 8, 768), F32),
            dma((3, 3, 3, 2)),
            dma((3, 3, 3, 2)),
            dma((3, 3)),
            dma((3, 3)),
            dma((5,)),
            dma((3, 3, 3)),
            dma((3, 3, 3)),
            dma((3,)),
        ],
        compiler_params=pltpu.CompilerParams(collective_id=0, has_side_effects=True, vmem_limit_bytes=48 * 2**20),
        name="gradient_sums",
    )(grads, small)


def normalize(values):
    center = values - jnp.mean(values, axis=-1, keepdims=True)
    inverse = lax.rsqrt(jnp.mean(center * center, axis=-1, keepdims=True) + epsilon)
    return (center * inverse, inverse)


def norm_back(grad_normed, normed, inverse):
    return inverse * (
        grad_normed
        - jnp.mean(grad_normed, axis=-1, keepdims=True)
        - normed * jnp.mean(grad_normed * normed, axis=-1, keepdims=True)
    )


def gelu_slope(values):
    return 0.5 * (1.0 + lax.erf(values * root_half)) + values * density_scale * jnp.exp(-0.5 * values * values)


def dot(a, b):
    return jnp.dot(a, b, preferred_element_type=F32)


def row_inner(a, b):
    return lax.dot_general(a, b, (((0,), (0,)), ((), ())), preferred_element_type=F32).astype(BF)


def back_product(a, b):
    return lax.dot_general(a, b, (((1,), (1,)), ((), ())), preferred_element_type=F32)


def both_cores(part):
    return part.astype(F32) + lax.ppermute(part, "section", [(0, 1), (1, 0)]).astype(F32)


def heads(a):
    return a.reshape(2, 256, 6, HEAD)


def layer_forward(x, flags, w):
    g1, b1, qkv_w, out_w, g2, b2, up_w, up_b, down_w, table = w
    bias = jnp.where(flags[:, None] == 0, table[0][None], table[1][None])
    shifted = (x.reshape(2, 256, -1) + bias[:, None]).reshape(512, -1)
    n1, i1 = normalize(shifted)
    a1 = (n1 * g1 + b1).astype(BF)
    q, k, v = (heads(dot(a1, qkv_w[i]).astype(BF)) for i in range(3))
    scores = jnp.einsum("bqhd,bkhd->bhqk", q, k, preferred_element_type=F32) * HEAD**-0.5
    top = jnp.max(scores, axis=-1, keepdims=True)
    lse = top + jnp.log(jnp.sum(jnp.exp(scores - top), axis=-1, keepdims=True))
    probs = jnp.exp(scores - lse)
    o = jnp.einsum("bhqk,bkhd->bqhd", probs.astype(BF), v, preferred_element_type=F32).astype(BF).reshape(512, -1)
    r = shifted + both_cores(dot(o, out_w).astype(BF))
    n2, i2 = normalize(r)
    a2 = (n2 * g2 + b2).astype(BF)
    u = dot(a2, up_w) + up_b
    g = jax.nn.gelu(u, approximate=False).astype(BF)
    out = r + both_cores(dot(g, down_w).astype(BF))
    return out, (n1, i1, a1, q, k, v, lse, o, n2, i2, a2, u, g)


def columns(a):
    return a.reshape(a.shape[0], -1, BC).transpose(1, 0, 2).reshape(-1, BR, BC)


def layer_backward(dy, kept, flags, w):
    g1, b1, qkv_w, out_w, g2, b2, up_w, up_b, down_w, table = w
    n1, i1, a1, q, k, v, lse, o, n2, i2, a2, u, g = kept
    dz = dy.astype(BF)
    grad_down = row_inner(g, dz)
    du = (back_product(dz, down_w) * gelu_slope(u)).astype(BF)
    grad_up_b = jnp.sum(du, axis=0, dtype=F32)
    grad_up = row_inner(a2, du)
    da2 = both_cores(back_product(du, up_w).astype(BF))
    grad_g2 = jnp.sum(da2 * n2, axis=0)
    grad_b2 = jnp.sum(da2, axis=0)
    dr = dy + norm_back(da2 * g2, n2, i2)
    dattn = dr.astype(BF)
    grad_out = row_inner(o, dattn)
    do = heads(back_product(dattn, out_w).astype(BF))
    scores = jnp.einsum("bqhd,bkhd->bhqk", q, k, preferred_element_type=F32) * HEAD**-0.5
    probs = jnp.exp(scores - lse)
    dprobs = jnp.einsum("bqhd,bkhd->bhqk", do, v, preferred_element_type=F32)
    dv = jnp.einsum("bhqk,bqhd->bkhd", probs.astype(BF), do, preferred_element_type=F32).astype(BF).reshape(512, -1)
    ds = (probs * (dprobs - jnp.sum(probs * dprobs, axis=-1, keepdims=True))).astype(BF)
    dq = (jnp.einsum("bhqk,bkhd->bqhd", ds, k, preferred_element_type=F32) * HEAD**-0.5).astype(BF).reshape(512, -1)
    dk = (jnp.einsum("bhqk,bqhd->bkhd", ds, q, preferred_element_type=F32) * HEAD**-0.5).astype(BF).reshape(512, -1)
    grad_qkv = [row_inner(a1, d) for d in (dq, dk, dv)]
    da1 = both_cores((back_product(dq, qkv_w[0]) + back_product(dk, qkv_w[1]) + back_product(dv, qkv_w[2])).astype(BF))
    grad_g1 = jnp.sum(da1 * n1, axis=0)
    grad_b1 = jnp.sum(da1, axis=0)
    dx = dr + norm_back(da1 * g1, n1, i1)
    cells = jnp.sum(dx.reshape(2, 256, -1), axis=1)
    grad_table = [jnp.sum(jnp.where(flags[:, None] == s, cells, 0.0), axis=0) for s in (0, 1)]
    small = jnp.concatenate([jnp.stack([grad_g1, grad_b1, grad_g2, grad_b2, *grad_table]), grad_up_b.reshape(2, 768)])
    blocks = jnp.stack(
        [
            columns(grad_down),
            columns(grad_up),
            jnp.concatenate([columns(d) for d in grad_qkv] + [columns(grad_out)]),
        ]
    )
    return dx, blocks, small


def shards(
    embeddings,
    species,
    ln1_gain,
    ln1_bias,
    qkv_weight,
    out_weight,
    ln2_gain,
    ln2_bias,
    up_weight,
    up_bias,
    down_weight,
    species_bias,
    out_cotangent,
):
    core = lax.axis_index("section")
    half = lax.axis_index("tensor")
    swap_cores = [(0, 1), (1, 0)]
    cross = [(0, 3), (1, 2), (2, 1), (3, 0)]
    own = (
        ln1_gain[0],
        ln1_bias[0],
        qkv_weight[0].transpose(1, 0, 2),
        out_weight[0],
        ln2_gain[0],
        ln2_bias[0],
        up_weight[0],
        up_bias[0],
        down_weight[0],
        species_bias[0],
    )
    split = (False, False, True, True, False, False, True, True, True, False)
    other = tuple(
        lax.ppermute(a, ("section", "tensor"), cross) if cut else lax.ppermute(a, "section", swap_cores)
        for a, cut in zip(own, split)
    )
    first = core == 0
    weights = (
        tuple(jnp.where(first, a, b) for a, b in zip(own, other)),
        tuple(jnp.where(first, b, a) for a, b in zip(own, other)),
    )
    cells = lax.dynamic_slice_in_dim(embeddings, half * 2, 2, 0).reshape(512, -1)
    flags = lax.dynamic_slice_in_dim(species, half * 2, 2, 0)
    cotangent = lax.dynamic_slice_in_dim(out_cotangent, half * 2, 2, 0).reshape(512, -1)
    out0, kept0 = layer_forward(cells.astype(F32), flags, weights[0])
    out1, kept1 = layer_forward(out0.astype(BF).astype(F32), flags, weights[1])
    dx1, blocks1, small1 = layer_backward(cotangent, kept1, flags, weights[1])
    dx0, blocks0, small0 = layer_backward(dx1.astype(BF).astype(F32), kept0, flags, weights[0])

    def four_cells(a0, a1):
        mine = jnp.where(first, a0, a1).astype(BF).reshape(2, 256, -1)
        theirs = lax.ppermute(mine, "tensor", swap_cores)
        low = half == 0
        return jnp.concatenate([jnp.where(low, mine, theirs), jnp.where(low, theirs, mine)]).astype(F32)[None]

    layer_out = four_cells(out0, out1)
    input_grad = four_cells(dx0, dx1)
    full, small = summed(jnp.stack([blocks0, blocks1]), jnp.stack([small0, small1]))

    def whole(blocks, rows):
        return blocks.reshape(-1, rows, BC).transpose(1, 0, 2).reshape(rows, -1).astype(F32)[None]

    grad_down = whole(full[0], 1536)
    grad_up = whole(full[1], 768)
    grad_qkv = full[2, :24].reshape(3, 768, BC).transpose(1, 0, 2).astype(F32)[None]
    grad_out = whole(full[2, 24:], 384)
    return (
        layer_out,
        input_grad,
        small[0:1],
        small[1:2],
        grad_qkv,
        grad_out,
        small[2:3],
        small[3:4],
        grad_up,
        small[6:8].reshape(1, 1536),
        grad_down,
        small[4:6][None],
    )


def solution(mesh):
    placed = (
        P("dp", None, None),
        P("dp"),
        P("section", None),
        P("section", None),
        P("section", None, None, "tensor"),
        P("section", "tensor", None),
        P("section", None),
        P("section", None),
        P("section", None, "tensor"),
        P("section", "tensor"),
        P("section", "tensor", None),
        P("section", None, None),
        P("dp", None, None),
    )
    return jax.shard_map(
        shards,
        mesh=mesh,
        in_specs=placed,
        out_specs=(
            P("section", "dp", None, None),
            P("section", "dp", None, None),
            P("section", None),
            P("section", None),
            P("section", None, None, "tensor"),
            P("section", "tensor", None),
            P("section", None),
            P("section", None),
            P("section", None, "tensor"),
            P("section", "tensor"),
            P("section", "tensor", None),
            P("section", None, None),
        ),
        check_vma=False,
    )
```

time: 1590 us -> 568 us (0.36)
  waiting for transfers between devices: 952 us -> 113 us
  blocking collectives: 159 us -> 0 us
  Pallas kernels: 0 us -> 135 us
  matrix products: 208 us -> 83.1 us
  other arithmetic: 117 us -> 78.1 us
  starting transfers between devices: 15.5 us -> 32.3 us
    psum x20 -> x0, waiting for transfers between devices: 952 us -> none  [the longest x1 458 us: shards(): lax.psum((head_totals[0], head_totals[1], head_totals[2], head_totals[3],...]
    psum x1 -> x0, blocking collectives: 159 us -> none  [shards(): lax.psum((head_totals[0], head_totals[1], head_totals[2], head_totals[3],...]
    pallas_call x0 -> x1, Pallas kernels: none -> 135 us  [summed(): pl.pallas_call(sum_kernel, out_shape=(jax.ShapeDtypeStruct((3, 32, BR, BC...]
    dot_general x95 -> x48, matrix products: 208 us -> 83.1 us  [the longest x12 34.8 us: dot(): return jnp.dot(a, b, preferred_element_type=F32)]
    ppermute x8 -> x20, waiting for transfers between devices: 0.02 us -> 113 us  [the longest x5 111 us: shards(): lax.ppermute(a, ('section', 'tensor'), cross)]
    unnamed x423 -> x253, local copies, waits for them, and re-layouts: 74 us -> 18.7 us
    convert_element_type x5 -> x22, local copies, waits for them, and re-layouts: 3.51 us -> 55.5 us  [the longest x6 37.9 us: whole(): blocks.reshape(-1, rows, BC).transpose(1, 0, 2).reshape(rows, -1)]
    reshape x0 -> x16, local copies, waits for them, and re-layouts: none -> 28.8 us  [the longest x8 14 us: heads(): return a.reshape(2, 256, 6, HEAD)]
  transfers between devices with their start and end apart: 28 -> 20, of which waited for: 20 -> 4; matrix products, arithmetic and copies ran while one was open for 12% -> 35% of each run, Pallas kernels for 0% -> 24%
where the time goes in v1:
time: 568 us; the launch traced here: 559 us
  Pallas kernels  135 us (24%)
  local copies, waits for them, and re-layouts  114 us (20%)
  waiting for transfers between devices  113 us (20%)
  matrix products  83.1 us (15%)
  other arithmetic  78.1 us (14%)
  starting transfers between devices  32.3 us (6%)
    pallas_call x1, Pallas kernels, summed(): pl.pallas_call(sum_kernel, out_shape=(jax.ShapeDtypeStruct((3, 32, BR, BC...  135 us
    ppermute x5, waiting for transfers between devices, shards(): lax.ppermute(a, ('section', 'tensor'), cross)  111 us
    convert_element_type x6, local copies, waits for them, and re-layouts, whole(): blocks.reshape(-1, rows, BC).transpose(1, 0, 2).reshape(rows, -1)  37.9 us
    dot_general x12, matrix products, dot(): return jnp.dot(a, b, preferred_element_type=F32)  34.8 us
    dot_general x12, matrix products, back_product(): lax.dot_general(a, b, (((1,), (1,)), ((), ())), preferred_element_type=F32)  20.5 us
    unnamed x253, local copies, waits for them, and re-layouts  18.7 us
    ppermute x8, starting transfers between devices, both_cores(): lax.ppermute(part, 'section', [(0, 1), (1, 0)]).astype(F32)  17.6 us
    reshape x8, local copies, waits for them, and re-layouts, heads(): return a.reshape(2, 256, 6, HEAD)  14 us
  transfers between devices with their start and end apart: 20, of which 4 were waited for; matrix products, arithmetic and copies ran while one was open for 35% of the time, Pallas kernels for 24%

profile of v1, /device:TPU:0, one launch (start us, length us, event | category | flops | bytes accessed | tf_op | source)
XLA Modules:
  0.0 558.6 jit_solution(2595059522607350993)
XLA Ops:
  0.7 3.5 collective-permute-start.8
  8.4 3.1 collective-permute-start.4
  18.2 2.7 convert_add_fusion.4
  20.9 73.1 %collective-permute-done.3 = bf16[3,768,384]{2,1,0:T(8,128)(2,1)} collective-permute-done((bf16[3,768,384]{2,1,0:T(8,128)(2,1)}, bf16[3,768,384]{2,1,0:T(8,128)(2,1)}, u32[]{:S(2)}, u32[]{:S(2)}) %collective-permute-start.3) | collective-permute-done | bytes 1769504 | tf_op jit(solution)/shard_map/ppermute | solution.py:373
  94.0 3.0 broadcast_select_fusion.4
  102.3 1.9 copy.59
  115.0 2.7 fusion.46
  119.7 2.3 collective-permute-start.5
  124.6 3.1 collective-permute-start.9
  133.8 2.4 fusion.116
  136.6 9.7 %fusion.2 = (bf16[512,1536]{1,0:T(8,128)(2,1)S(1)}, f32[512,1536]{1,0:T(8,128)}) fusion(f32[1536]{0:T(1024)S(1)} %get-tuple-element.71, bf16[768,1536]{1,0:T(8,128)(2,1)} %collective-permute-done.8, pred[]{:T(512)S(6)} %eq.20, bf16[1,768,1536]{2,1,0:T(8,128)(2,1)S(1)} %copy-done.110, f32[512,768]{1,0:T(8,128)S(1)} %get-tuple-element.51, ...), kind=kOutput, calls=%fused_computation.20 | convolution fusion | flops 1263009792 | bytes 11026433 | tf_op jit(solution)/shard_map/dot_general | solution.py:256
  146.3 37.6 %collective-permute-done.10 = bf16[1536,768]{1,0:T(8,128)(2,1)S(1)} collective-permute-done((bf16[1536,768]{1,0:T(8,128)(2,1)}, bf16[1536,768]{1,0:T(8,128)(2,1)S(1)}, u32[]{:S(2)}, u32[]{:S(2)}) %collective-permute-start.10) | collective-permute-done | bytes 2359328 | tf_op jit(solution)/shard_map/ppermute | solution.py:373
  209.7 2.7 convolution_convert_fusion.8
  212.4 10.5 %collective-permute-start.12 = (bf16[512,768]{1,0:T(8,128)(2,1)}, bf16[512,768]{1,0:T(8,128)(2,1)}, u32[]{:S(2)}, u32[]{:S(2)}) collective-permute-start(bf16[512,768]{1,0:T(8,128)(2,1)} %convolution_convert_fusion.8), channel_id=1, source_target_pairs={{0,64},{64,0},{1,65},{65,1},{2,66},{66,2},{3,67},{67,3},{4,68},{68... | collective-permute-start | bytes 2359304 | tf_op jit(solution)/shard_map/ppermute | solution.py:268
  227.8 9.9 %fusion.5 = (bf16[512,1536]{1,0:T(8,128)(2,1)S(1)}, f32[512,1536]{1,0:T(8,128)S(1)}) fusion(f32[1536]{0:T(1024)S(1)} %copy-done.100, bf16[768,1536]{1,0:T(8,128)(2,1)} %collective-permute-done.8, pred[]{:T(512)S(6)} %eq.20, bf16[1,768,1536]{2,1,0:T(8,128)(2,1)S(1)} %copy-done.111, f32[512,768]{1,0:T(8,128)S(1)} %get-tuple-element.47, ...), kind=kOutput, calls=%fused_computation.23 | convolution fusion | flops 1263009792 | bytes 11026433 | tf_op jit(solution)/shard_map/dot_general | solution.py:256
  237.7 3.3 convert_reduce_fusion
  241.0 4.0 convolution_convert_fusion.5
  244.9 2.3 convolution_convert_fusion.6
  251.0 2.9 convolution_convert_fusion.1
  253.9 4.5 copy.101
  259.8 2.8 multiply_reduce_fusion.4
  262.7 2.2 bitcast_add_fusion
  266.1 2.6 convolution_convert_fusion.21
  268.7 1.9 copy.74
  272.4 2.1 multiply_reduce_fusion.1
  290.3 3.3 convert_reduce_fusion.1
  293.6 2.4 convolution_convert_fusion.4
  296.0 2.3 collective-permute-start.17
  298.3 3.5 maximum_bitcast_fusion.1
  304.7 2.8 convolution_convert_fusion.3
  309.2 4.3 copy.98
  317.4 2.9 multiply_reduce_fusion.6
  320.4 3.6 multiply_add_fusion.1
  330.3 2.0 multiply_reduce_fusion
  348.8 5.9 %pad_maximum_fusion.g_ref = bf16[2,3,32,96,384]{4,3,2,1,0:T(8,128)(2,1)} fusion(bf16[1,3,32,96,384]{4,3,2,1,0:T(8,128)(2,1)S(1)} %bitcast.347, bf16[1,3,32,96,384]{4,3,2,1,0:T(8,128)(2,1)S(1)} %maximum_bitcast_fusion), kind=kLoop, calls=%fused_computation | loop fusion | flops 7077888 | bytes 28311552 | tf_op jit(solution)/shard_map/stack | solution.py:397
  357.7 134.7 %gradient_sums.1 = (bf16[3,32,96,384]{3,2,1,0:T(8,128)(2,1)}, f32[8,768]{1,0:T(8,128)S(1)}) custom-call(bf16[2,3,32,96,384]{4,3,2,1,0:T(8,128)(2,1)} %pad_maximum_fusion.g_ref, f32[2,8,768]{2,1,0:T(8,128)S(1)} %pad_maximum_fusion.1.s_ref), custom_call_target="tpu_custom_call" | custom-call | tf_op jit(solution)/shard_map/gradient_sums/pallas_call | solution.py:207
  493.6 3.0 fusion.117
  497.6 2.0 collective-permute-start.19
  499.6 2.5 convert_bitcast_fusion.1
  502.2 2.4 convert_bitcast_fusion
  504.6 2.6 select_bitcast_fusion.3
  510.4 2.0 reshape.586
  512.4 7.5 %copy.105 = f32[768,4,384]{2,1,0:T(4,128)} copy(f32[768,4,384]{2,0,1:T(8,128)} %convert_bitcast_fusion.1) | data formatting | bytes 9437184 | tf_op jit(solution)/shard_map/convert_element_type | solution.py:400
  519.9 6.6 %reshape.587 = f32[1,768,1536]{2,1,0:T(8,128)} reshape(f32[768,4,384]{2,1,0:T(4,128)} %copy.105) | data formatting | bytes 9437184 | tf_op jit(solution)/shard_map/convert_element_type | solution.py:400
  527.1 13.7 %copy.106 = f32[1536,2,384]{2,1,0:T(2,128)} copy(f32[1536,2,384]{2,0,1:T(8,128)} %convert_bitcast_fusion) | data formatting | bytes 9437184 | tf_op jit(solution)/shard_map/convert_element_type | solution.py:400
  540.8 7.2 %reshape.588 = f32[1,1536,768]{2,1,0:T(8,128)} reshape(f32[1536,2,384]{2,1,0:T(2,128)} %copy.106) | data formatting | bytes 9437184 | tf_op jit(solution)/shard_map/convert_element_type | solution.py:400
  548.0 3.0 maximum_convert_fusion
  551.6 2.0 convert_bitcast_fusion.2
  (425 shorter events, 136.8 us)
Async XLA Ops:
  0.6 222.3 %copy-start = (f32[4,256,768]{2,1,0:T(8,128)S(1)}, f32[4,256,768]{2,1,0:T(8,128)}, u32[]{:S(2)}) copy-start(f32[4,256,768]{2,1,0:T(8,128)} %param.25) | copy-start | bytes 9437188
  0.7 135.9 %collective-permute-start.8 = (bf16[768,1536]{1,0:T(8,128)(2,1)}, bf16[768,1536]{1,0:T(8,128)(2,1)}, u32[]{:S(2)}, u32[]{:S(2)}) collective-permute-start(bf16[768,1536]{1,0:T(8,128)(2,1)} %bitcast.411), channel_id=1, source_target_pairs={{0,65},{1,64},{64,1},{65,0},{2,67},{3,66},{66,3},{67,2},{4,69},{5,... | collective-permute-start | bytes 7077896 | tf_op jit(solution)/shard_map/ppermute | solution.py:373
  4.1 8.5 %collective-permute-start = (f32[2,768]{1,0:T(2,128)}, f32[2,768]{1,0:T(2,128)S(1)}, u32[]{:S(2)}, u32[]{:S(2)}) collective-permute-start(f32[2,768]{1,0:T(2,128)} %bitcast.409), channel_id=1, source_target_pairs={{0,64},{64,0},{1,65},{65,1},{2,66},{66,2},{3,67},{67,3},{4,68},{68... | collective-permute-start | bytes 18440 | tf_op jit(solution)/shard_map/ppermute | solution.py:373
  5.5 2.8 collective-permute-start.2
  6.3 5.7 %collective-permute-start.1 = (f32[768]{0:T(1024)S(1)}, f32[768]{0:T(1024)S(1)}, u32[]{:S(2)}, u32[]{:S(2)}) collective-permute-start(f32[768]{0:T(1024)S(1)} %reduce.4), channel_id=1, source_target_pairs={{0,64},{64,0},{1,65},{65,1},{2,66},{66,2},{3,67},{67,3},{4,68},{68... | collective-permute-start | bytes 9224 | tf_op jit(solution)/shard_map/ppermute | solution.py:373
  6.9 87.1 %collective-permute-start.3 = (bf16[3,768,384]{2,1,0:T(8,128)(2,1)}, bf16[3,768,384]{2,1,0:T(8,128)(2,1)}, u32[]{:S(2)}, u32[]{:S(2)}) collective-permute-start(bf16[3,768,384]{2,1,0:T(8,128)(2,1)} %bitcast.389), channel_id=1, source_target_pairs={{0,65},{1,64},{64,1},{65,0},{2,67},{3,66},{66,3},{67,2},{4,69},{5,... | collective-permute-start | bytes 5308424 | tf_op jit(solution)/shard_map/ppermute | solution.py:373
  8.3 12.5 %copy-start.101 = (pred[2]{0:T(512)(128)(4,1)}, pred[2]{0:T(512)(128)(4,1)S(1)}, u32[]{:S(2)}) copy-start(pred[2]{0:T(512)(128)(4,1)S(1)} %get-tuple-element.87) | copy-start | bytes 10
  8.4 109.8 %collective-permute-start.4 = (bf16[384,768]{1,0:T(8,128)(2,1)}, bf16[384,768]{1,0:T(8,128)(2,1)}, u32[]{:S(2)}, u32[]{:S(2)}) collective-permute-start(bf16[384,768]{1,0:T(8,128)(2,1)} %bitcast.388), channel_id=1, source_target_pairs={{0,65},{1,64},{64,1},{65,0},{2,67},{3,66},{66,3},{67,2},{4,69},{5,... | collective-permute-start | bytes 1769480 | tf_op jit(solution)/shard_map/ppermute | solution.py:373
  12.6 8.3 %copy-start.61 = (f32[768]{0:T(1024)}, f32[768]{0:T(1024)S(1)}, u32[]{:S(2)}) copy-start(f32[768]{0:T(1024)S(1)} %get-tuple-element.79) | copy-start | bytes 9220
  14.0 80.0 %copy-start.50 = (bf16[1,768,3,384]{3,1,2,0:T(8,128)(2,1)S(1)}, bf16[1,768,3,384]{3,1,2,0:T(8,128)(2,1)}, u32[]{:S(2)}) copy-start(bf16[1,768,3,384]{3,1,2,0:T(8,128)(2,1)} %param.17) | copy-start | bytes 5308420
  20.9 78.0 %copy-start.22 = (bf16[2,256,768]{2,1,0:T(8,128)(2,1)}, bf16[2,256,768]{2,1,0:T(8,128)(2,1)S(1)}, u32[]{:S(2)}) copy-start(bf16[2,256,768]{2,1,0:T(8,128)(2,1)S(1)} %get-tuple-element.57) | copy-start | bytes 2359300
  119.7 14.1 %collective-permute-start.5 = (bf16[512,768]{1,0:T(8,128)(2,1)}, bf16[512,768]{1,0:T(8,128)(2,1)}, u32[]{:S(2)}, u32[]{:S(2)}) collective-permute-start(bf16[512,768]{1,0:T(8,128)(2,1)} %convolution_convert_fusion.9), channel_id=1, source_target_pairs={{0,64},{64,0},{1,65},{65,1},{2,66},{66,2},{3,67},{67,3},{4,68},{68... | collective-permute-start | bytes 2359304 | tf_op jit(solution)/shard_map/ppermute | solution.py:268
  123.3 5.7 %collective-permute-start.7 = (f32[768]{0:T(1024)}, f32[768]{0:T(1024)}, u32[]{:S(2)}, u32[]{:S(2)}) collective-permute-start(f32[768]{0:T(1024)} %reduce.7), channel_id=1, source_target_pairs={{0,64},{64,0},{1,65},{65,1},{2,66},{66,2},{3,67},{67,3},{4,68},{68... | collective-permute-start | bytes 9224 | tf_op jit(solution)/shard_map/ppermute | solution.py:373
  124.6 7.9 %collective-permute-start.9 = (f32[1536]{0:T(1024)}, f32[1536]{0:T(1024)}, u32[]{:S(2)}, u32[]{:S(2)}) collective-permute-start(f32[1536]{0:T(1024)} %reduce.8), channel_id=1, source_target_pairs={{0,65},{1,64},{64,1},{65,0},{2,67},{3,66},{66,3},{67,2},{4,69},{5,... | collective-permute-start | bytes 18440 | tf_op jit(solution)/shard_map/ppermute | solution.py:373
  129.0 2.2 collective-permute-start.6
  129.0 54.9 %collective-permute-start.10 = (bf16[1536,768]{1,0:T(8,128)(2,1)}, bf16[1536,768]{1,0:T(8,128)(2,1)S(1)}, u32[]{:S(2)}, u32[]{:S(2)}) collective-permute-start(bf16[1536,768]{1,0:T(8,128)(2,1)} %bitcast.410), channel_id=1, source_target_pairs={{0,65},{1,64},{64,1},{65,0},{2,67},{3,66},{66,3},{67,2},{4,69},{5,... | collective-permute-start | bytes 7077896 | tf_op jit(solution)/shard_map/ppermute | solution.py:373
  131.2 5.3 copy-start.103
  136.2 51.6 %copy-start.6 = (f32[512,768]{1,0:T(8,128)}, f32[512,768]{1,0:T(8,128)S(1)}, u32[]{:S(2)}) copy-start(f32[512,768]{1,0:T(8,128)S(1)} %get-tuple-element.51) | copy-start | bytes 4718596
  136.2 10.1 %copy-start.72 = (f32[512]{0:T(512)}, f32[512]{0:T(512)S(1)}, u32[]{:S(2)}) copy-start(f32[512]{0:T(512)S(1)} %broadcast_multiply_fusion.10) | copy-start | bytes 6148
  136.5 9.8 %copy-start.84 = (f32[512]{0:T(512)}, f32[512]{0:T(512)S(1)}, u32[]{:S(2)}) copy-start(f32[512]{0:T(512)S(1)} %add_rsqrt_fusion.2) | copy-start | bytes 6148
  136.6 47.3 %copy-start.107 = (bf16[1,1536,768]{2,1,0:T(8,128)(2,1)S(1)}, bf16[1,1536,768]{2,1,0:T(8,128)(2,1)}, u32[]{:S(2)}) copy-start(bf16[1,1536,768]{2,1,0:T(8,128)(2,1)} %param.23) | copy-start | bytes 7077892
  146.3 39.0 %copy-start.116 = (bf16[512,1536]{1,0:T(8,128)(2,1)}, bf16[512,1536]{1,0:T(8,128)(2,1)S(1)}, u32[]{:S(2)}) copy-start(bf16[512,1536]{1,0:T(8,128)(2,1)S(1)} %get-tuple-element.92) | copy-start | bytes 4718596
  185.3 2.4 collective-permute-start.11
  212.4 13.1 %collective-permute-start.12 = (bf16[512,768]{1,0:T(8,128)(2,1)}, bf16[512,768]{1,0:T(8,128)(2,1)}, u32[]{:S(2)}, u32[]{:S(2)}) collective-permute-start(bf16[512,768]{1,0:T(8,128)(2,1)} %convolution_convert_fusion.8), channel_id=1, source_target_pairs={{0,64},{64,0},{1,65},{65,1},{2,66},{66,2},{3,67},{67,3},{4,68},{68... | collective-permute-start | bytes 2359304 | tf_op jit(solution)/shard_map/ppermute | solution.py:268
  227.4 35.3 %copy-start.8 = (f32[512,768]{1,0:T(8,128)}, f32[512,768]{1,0:T(8,128)S(1)}, u32[]{:S(2)}) copy-start(f32[512,768]{1,0:T(8,128)S(1)} %get-tuple-element.47) | copy-start | bytes 4718596
  227.4 20.4 %copy-start.75 = (f32[512]{0:T(512)}, f32[512]{0:T(512)S(1)}, u32[]{:S(2)}) copy-start(f32[512]{0:T(512)S(1)} %broadcast_multiply_fusion.8) | copy-start | bytes 6148
  227.7 20.1 %copy-start.87 = (f32[512]{0:T(512)}, f32[512]{0:T(512)S(1)}, u32[]{:S(2)}) copy-start(f32[512]{0:T(512)S(1)} %add_rsqrt_fusion) | copy-start | bytes 6148
  227.7 9.9 %copy-start.108 = (bf16[1,1536,768]{2,1,0:T(8,128)(2,1)S(1)}, bf16[1,1536,768]{2,1,0:T(8,128)(2,1)}, u32[]{:S(2)}) copy-start(bf16[1,1536,768]{2,1,0:T(8,128)(2,1)} %param.23) | copy-start | bytes 7077892
  227.8 9.9 %copy-start.114 = (bf16[1536,768]{1,0:T(8,128)(2,1)S(1)}, bf16[1536,768]{1,0:T(8,128)(2,1)}, u32[]{:S(2)}) copy-start(bf16[1536,768]{1,0:T(8,128)(2,1)} %copy-done.113) | copy-start | bytes 7077892
  244.9 14.9 %collective-permute-start.15 = (bf16[512,768]{1,0:T(8,128)(2,1)}, bf16[512,768]{1,0:T(8,128)(2,1)}, u32[]{:S(2)}, u32[]{:S(2)}) collective-permute-start(bf16[512,768]{1,0:T(8,128)(2,1)} %convolution_convert_fusion.5), channel_id=1, source_target_pairs={{0,64},{64,0},{1,65},{65,1},{2,66},{66,2},{3,67},{67,3},{4,68},{68... | collective-permute-start | bytes 2359304 | tf_op jit(solution)/shard_map/ppermute | solution.py:268
  247.2 73.1 %collective-permute-start.13 = (bf16[512,768]{1,0:T(8,128)(2,1)}, bf16[512,768]{1,0:T(8,128)(2,1)}, u32[]{:S(2)}, u32[]{:S(2)}) collective-permute-start(bf16[512,768]{1,0:T(8,128)(2,1)} %convolution_convert_fusion.6), channel_id=1, source_target_pairs={{0,64},{64,0},{1,65},{65,1},{2,66},{66,2},{3,67},{67,3},{4,68},{68... | collective-permute-start | bytes 2359304 | tf_op jit(solution)/shard_map/ppermute | solution.py:268
  266.1 6.3 %copy-start.5 = (f32[2,6,256,256]{2,3,1,0:T(8,128)S(1)}, f32[2,6,256,256]{2,3,1,0:T(8,128)}, u32[]{:S(2)}) copy-start(f32[2,6,256,256]{2,3,1,0:T(8,128)} %copy-done.4) | copy-start | bytes 9437188
  282.9 2.9 collective-permute-start.16
  289.4 15.3 %copy-start.32 = (bf16[512,768]{1,0:T(8,128)(2,1)}, bf16[512,768]{1,0:T(8,128)(2,1)S(1)}, u32[]{:S(2)}) copy-start(bf16[512,768]{1,0:T(8,128)(2,1)S(1)} %get-tuple-element.45) | copy-start | bytes 2359300
  296.0 21.5 %collective-permute-start.17 = (bf16[512,768]{1,0:T(8,128)(2,1)}, bf16[512,768]{1,0:T(8,128)(2,1)}, u32[]{:S(2)}, u32[]{:S(2)}) collective-permute-start(bf16[512,768]{1,0:T(8,128)(2,1)} %convolution_convert_fusion.4), channel_id=1, source_target_pairs={{0,64},{64,0},{1,65},{65,1},{2,66},{66,2},{3,67},{67,3},{4,68},{68... | collective-permute-start | bytes 2359304 | tf_op jit(solution)/shard_map/ppermute | solution.py:268
  298.3 4.7 copy-start.7
  298.3 4.7 copy-start.68
  313.5 6.9 %copy-start.9 = (f32[512,768]{1,0:T(8,128)S(1)}, f32[512,768]{1,0:T(8,128)}, u32[]{:S(2)}) copy-start(f32[512,768]{1,0:T(8,128)} %copy-done.8) | copy-start | bytes 4718596
  320.4 4.9 copy-start.49
  325.2 5.1 copy-start.3
  340.6 164.0 %collective-permute-start.14 = (bf16[2,256,768]{2,1,0:T(8,128)(2,1)}, bf16[2,256,768]{2,1,0:T(8,128)(2,1)}, u32[]{:S(2)}, u32[]{:S(2)}) collective-permute-start(bf16[2,256,768]{2,1,0:T(8,128)(2,1)} %bitcast.18), channel_id=1, source_target_pairs={{0,1},{1,0},{2,3},{3,2},{4,5},{5,4},{6,7},{7,6},{8,9},{9,8},{10,11... | collective-permute-start | bytes 2359304 | tf_op jit(solution)/shard_map/ppermute | solution.py:391
  343.0 11.7 %collective-permute-start.18 = (bf16[512,768]{1,0:T(8,128)(2,1)S(1)}, bf16[512,768]{1,0:T(8,128)(2,1)S(1)}, u32[]{:S(2)}, u32[]{:S(2)}) collective-permute-start(bf16[512,768]{1,0:T(8,128)(2,1)S(1)} %add_convert_fusion), channel_id=1, source_target_pairs={{0,64},{64,0},{1,65},{65,1},{2,66},{66,2},{3,67},{67,3},{4,68},{68... | collective-permute-start | bytes 2359304 | tf_op jit(solution)/shard_map/ppermute | solution.py:268
  348.8 5.9 %copy-start.13 = (f32[2,256,768]{2,1,0:T(8,128)S(1)}, f32[2,256,768]{2,1,0:T(8,128)}, u32[]{:S(2)}) copy-start(f32[2,256,768]{2,1,0:T(8,128)} %get-tuple-element.56) | copy-start | bytes 4718596
  348.8 5.9 %copy-start.62 = (f32[768]{0:T(1024)S(1)}, f32[768]{0:T(1024)}, u32[]{:S(2)}) copy-start(f32[768]{0:T(1024)} %copy-done.61) | copy-start | bytes 9220
  348.8 6.0 %copy-start.82 = (f32[1,2,2,128]{3,1,2,0:T(2,128)S(1)}, f32[1,2,2,128]{3,1,2,0:T(2,128)}, u32[]{:S(2)}) copy-start(f32[1,2,2,128]{3,1,2,0:T(2,128)} %copy.128) | copy-start | bytes 6148
  348.8 6.0 %copy-start.83 = (f32[1,2,2,128]{3,1,2,0:T(2,128)S(1)}, f32[1,2,2,128]{3,1,2,0:T(2,128)}, u32[]{:S(2)}) copy-start(f32[1,2,2,128]{3,1,2,0:T(2,128)} %copy.124) | copy-start | bytes 6148
  497.6 56.1 %collective-permute-start.19 = (bf16[2,256,768]{2,1,0:T(8,128)(2,1)}, bf16[2,256,768]{2,1,0:T(8,128)(2,1)}, u32[]{:S(2)}, u32[]{:S(2)}) collective-permute-start(bf16[2,256,768]{2,1,0:T(8,128)(2,1)} %bitcast.28), channel_id=1, source_target_pairs={{0,1},{1,0},{2,3},{3,2},{4,5},{5,4},{6,7},{7,6},{8,9},{9,8},{10,11... | collective-permute-start | bytes 2359304 | tf_op jit(solution)/shard_map/ppermute | solution.py:391
  540.8 7.2 %copy-start.45 = (bf16[1,2,256,768]{3,2,1,0:T(8,128)(2,1)S(1)}, bf16[1,2,256,768]{3,2,1,0:T(8,128)(2,1)}, u32[]{:S(2)}) copy-start(bf16[1,2,256,768]{3,2,1,0:T(8,128)(2,1)} %get-tuple-element.62) | copy-start | bytes 2359300
  (93 other events, 217.2 us)
